TPU v7x, 32 devices: a whole 2x2x4 slice. The times are simulated.
32 devices in a mesh: group: 2 (over y), tensor: 16 (over z, x, core).
Axes of the slice: x: 2, y: 2, z: 4, core: 2. Of those that a mesh axis runs over, the one named last changes fastest.
Arguments:
- tokens: bfloat16 [512, 8192], P('group', 'tensor'), parts along dimension 0, may hold values from -480 to 480, as said below
- norm_gain: float32 [8192], replicated, may hold values from 0.5 to 1.5
- gate_levels: bfloat16 [8192, 26624], P(None, 'tensor'), may hold values from -8 to 7, as said below
- gate_scale: float32 [26624], P('tensor'), may hold values from 0.0012 to 0.0048
- up_levels: bfloat16 [8192, 26624], P(None, 'tensor'), may hold values from -8 to 7, as said below
- up_scale: float32 [26624], P('tensor'), may hold values from 0.0012 to 0.0048
- odd_factor: float32 [13, 13], replicated, may hold values from -1.75 to 1.75
- down_levels: bfloat16 [26624, 8192], P('tensor'), may hold values from -8 to 7, as said below
- down_scale: float32 [8192], P('tensor'), may hold values from 0.0013 to 0.005
Outputs:
- mixed: bfloat16 [512, 8192], P('group', 'tensor'), parts along dimension 0
There are 2 independent parts, one for each index of `group`. A program takes and returns all parts, laid end to end along the dimension named above; an argument that names none is the same for every part. Nothing has to cross between parts.
Inputs may be any that keep to these rules, and one draw needn't show every extreme that they name: `tokens`: row and column scales vary. `gate_levels`: whole numbers. `up_levels`: whole numbers. `down_levels`: whole numbers.
All inputs are finite; a program needn't handle non-finite values.
Results may differ from a plain program's by a relative error of at most 0.0071.
Values may be sent and summed in bfloat16 or wider, within the bound.
A program may use at most 384 MiB of HBM per device.

v0:
```python
import math

import jax
import jax.numpy as jnp
from jax import lax
from jax.sharding import PartitionSpec as P


def partner_2(block, axis, distance):
    count = lax.axis_size(axis)
    route = []
    for low in range(count):
        high = low | 1 << distance
        if high != low and high < count:
            route += [(low, high), (high, low)]
    return lax.ppermute(block, axis, route)


def sign_table(order):
    indices = jnp.arange(order, dtype=jnp.int32)
    common_bits = jnp.bitwise_and(indices[:, None], indices[None, :])
    parity = jnp.zeros((order, order), jnp.int32)
    for bit_index in range(max(1, order.bit_length())):
        parity = parity + jnp.bitwise_and(jnp.right_shift(common_bits, bit_index), 1)
    return (1 - 2 * jnp.bitwise_and(parity, 1)).astype(jnp.float32)


def shards(
    tokens,
    norm_gain,
    gate_levels,
    gate_scale,
    up_levels,
    up_scale,
    odd_factor,
    down_levels,
    down_scale,
):
    devices = lax.axis_size("tensor")
    gathered = lax.all_gather(tokens, "tensor", axis=1, tiled=True)
    floats = gathered.astype(jnp.float32)
    inverse = lax.rsqrt(jnp.mean(floats * floats, axis=1, keepdims=True) + 1e-05)
    normed = (floats * inverse * norm_gain).astype(jnp.bfloat16)
    gate_out = jnp.dot(normed, gate_levels, preferred_element_type=jnp.float32) * gate_scale
    up_out = jnp.dot(normed, up_levels, preferred_element_type=jnp.float32) * up_scale
    hidden = (jax.nn.silu(gate_out) * up_out).astype(jnp.bfloat16)
    odd_order = odd_factor.shape[0]
    hidden_width = hidden.shape[1]
    local_order = hidden_width // odd_order
    local_mixer = jnp.kron(sign_table(local_order), odd_factor.T)
    spread = jnp.dot(hidden.astype(jnp.float32), local_mixer, precision=lax.Precision.HIGHEST)
    position = lax.axis_index("tensor")
    for bit_index in range(devices.bit_length() - 1):
        partner = partner_2(spread, "tensor", bit_index)
        is_upper = jnp.bitwise_and(jnp.right_shift(position, bit_index), 1) == 1
        spread = jnp.where(is_upper, partner - spread, spread + partner)
    walsh_scale = 1.0 / math.sqrt(local_order * devices)
    rotated = (spread * walsh_scale).astype(jnp.bfloat16)
    partials = jnp.dot(rotated, down_levels, preferred_element_type=jnp.float32)
    summed = lax.psum_scatter(partials, "tensor", scatter_dimension=1, tiled=True)
    return (summed * down_scale).astype(jnp.bfloat16)


def solution(mesh):
    placed = (
        P("group", "tensor"),
        P(),
        P(None, "tensor"),
        P("tensor"),
        P(None, "tensor"),
        P("tensor"),
        P(),
        P("tensor", None),
        P("tensor"),
    )
    return jax.shard_map(
        shards, mesh=mesh, in_specs=placed, out_specs=P("group", "tensor"), check_vma=False
    )
```

profile of v0, /device:TPU:0, one launch (start us, length us, event | category | flops | bytes accessed | tf_op | source)
XLA Modules:
  0.0 450.3 jit_solution(9587140233092850819)
XLA Ops:
  6.5 0.7 all-gather.2.cloned.1.call-update
  7.3 0.8 copy.11
  8.1 0.1 subtract_convert_fusion
  8.2 34.5 %broadcast_multiply_fusion = f32[128,13,128,13]{3,2,1,0:T(8,128)} fusion(f32[13,13]{1,0:T(8,128)S(1)} %copy.11, f32[128,128]{1,0:T(8,128)S(1)} %subtract_convert_fusion), kind=kLoop, calls=%fused_computation | loop fusion | flops 2768896 | bytes 11141796 | tf_op jit(solution)/shard_map/jit(kron)/mul | solution.py:50
  42.7 71.0 %mul.102 = f32[1664,1664]{1,0:T(8,128)} reshape(f32[128,13,128,13]{3,2,1,0:T(8,128)} %broadcast_multiply_fusion) | data formatting | bytes 22151168 | tf_op jit(solution)/shard_map/jit(kron)/mul | solution.py:50
  113.7 3.3 fusion
  117.0 0.2 copy-done
  117.1 13.3 %convolution_multiply_fusion.1 = f32[256,1664]{1,0:T(8,128)S(1)} fusion(bf16[8192,1664]{1,0:T(8,128)(2,1)} %param.11, bf16[256,8192]{1,0:T(8,128)(2,1)S(1)} %copy-done, f32[8192]{0:T(1024)S(1)} %copy-done.2, f32[256]{0:T(256)S(1)} %add_rsqrt_fusion, f32[1664]{0:T(1024)S(1)} %copy-done.3), kind=kOutput, calls=%fused_computation.8 | convolution fusion | flops 6988136448 | bytes 33201664 | tf_op jit(solution)/shard_map/dot_general | solution.py:44
  130.5 18.8 %fusion.4 = bf16[256,1664]{1,0:T(8,128)(2,1)} fusion(bf16[8192,1664]{1,0:T(8,128)(2,1)} %param.13, f32[256,1664]{1,0:T(8,128)S(1)} %convolution_multiply_fusion.1, bf16[256,8192]{1,0:T(8,128)(2,1)} %all-gather.2.cloned.1.call-done, f32[8192]{0:T(1024)S(1)} %copy-done.2, f32[256]{0:T(256)S(1)} %add_rsqrt_fusion, f32[1664]{0:T(1024)S(1)} %copy-done.4), kind=kOutput, calls=%fused_computation.9 | convolution fusion | flops 6990692352 | bytes 34053632 | tf_op jit(solution)/shard_map/dot_general | solution.py:45
  149.3 7.0 %fusion.11 = f32[256,1664]{1,0:T(8,128)S(1)} fusion(bf16[256,1664]{1,0:T(8,128)(2,1)} %fusion.4, f32[1664,1664]{1,0:T(8,128)S(1)} %bitcast.9), kind=kOutput, calls=%fused_computation.21 | convolution fusion | flops 8506048512 | bytes 13631488 | tf_op jit(solution)/shard_map/dot_general | solution.py:51
  156.3 0.6 collective-permute-start
  156.9 3.4 collective-permute-done
  160.3 2.8 add_select_fusion.2
  163.1 2.8 collective-permute-start.1
  165.9 37.7 %collective-permute-done.1 = f32[256,1664]{1,0:T(8,128)S(1)} collective-permute-done((f32[256,1664]{1,0:T(8,128)}, f32[256,1664]{1,0:T(8,128)S(1)}, u32[]{:S(2)}, u32[]{:S(2)}) %collective-permute-start.1) | collective-permute-done | bytes 1703968 | tf_op jit(solution)/shard_map/ppermute | solution.py:16
  203.6 1.6 add_select_fusion.1
  205.3 1.9 collective-permute-start.2
  207.2 37.0 %collective-permute-done.2 = f32[256,1664]{1,0:T(8,128)} collective-permute-done((f32[256,1664]{1,0:T(8,128)S(1)}, f32[256,1664]{1,0:T(8,128)}, u32[]{:S(2)}, u32[]{:S(2)}) %collective-permute-start.2) | collective-permute-done | bytes 1703968 | tf_op jit(solution)/shard_map/ppermute | solution.py:16
  244.2 1.6 add_select_fusion
  245.8 2.6 collective-permute-start.3
  248.4 72.7 %collective-permute-done.3 = f32[256,1664]{1,0:T(8,128)S(1)} collective-permute-done((f32[256,1664]{1,0:T(8,128)S(1)}, f32[256,1664]{1,0:T(8,128)S(1)}, u32[]{:S(2)}, u32[]{:S(2)}) %collective-permute-start.3) | collective-permute-done | bytes 1703968 | tf_op jit(solution)/shard_map/ppermute | solution.py:16
  321.1 14.8 %fusion.7 = f32[256,8192]{1,0:T(8,128)} fusion(bf16[1664,8192]{1,0:T(8,128)(2,1)} %param.16, f32[256,1664]{1,0:T(8,128)S(1)} %add_select_fusion, f32[256,1664]{1,0:T(8,128)S(1)} %collective-permute-done.3, pred[]{:T(512)S(6)} %eq.12), kind=kOutput, calls=%fused_computation.14 | convolution fusion | flops 6981451776 | bytes 39059456 | tf_op jit(solution)/shard_map/dot_general | solution.py:59
  335.9 105.8 %reduce-scatter.2.cloned.1.call-done = f32[256,512]{1,0:T(8,128)} async-done(((f32[256,8192]{1,0:T(8,128)}), f32[256,512]{1,0:T(8,128)}) %reduce-scatter.2.cloned.1.call-update) | async-done | bytes 524304 | tf_op jit(solution)/shard_map/reduce_scatter | solution.py:60
  441.7 1.8 multiply_convert_fusion.2
  (21 shorter events, 0.1 us)
Async XLA Ops:
  6.5 107.1 %all-gather.2.cloned.1.call-start = ((), (), s32[]{:S(2)}) async-start(), calls=%async_computation.1 | async-start | bytes 4456448 | tf_op jit(solution)/shard_map/all_gather | solution.py:40
  7.3 434.4 %reduce-scatter.2.cloned.1.call-start = ((), (), s32[]{:S(2)}) async-start(), calls=%async_computation.2 | async-start | bytes 8912896 | tf_op jit(solution)/shard_map/reduce_scatter | solution.py:60
  42.7 74.3 %copy-start.2 = (f32[8192]{0:T(1024)S(1)}, f32[8192]{0:T(1024)}, u32[]{:S(2)}) copy-start(f32[8192]{0:T(1024)} %param.10) | copy-start | bytes 98308
  42.7 74.3 %copy-start.3 = (f32[1664]{0:T(1024)S(1)}, f32[1664]{0:T(1024)}, u32[]{:S(2)}) copy-start(f32[1664]{0:T(1024)} %param.12) | copy-start | bytes 19972
  113.7 3.4 copy-start
  117.1 13.3 %copy-start.4 = (f32[1664]{0:T(1024)S(1)}, f32[1664]{0:T(1024)}, u32[]{:S(2)}) copy-start(f32[1664]{0:T(1024)} %param.14) | copy-start | bytes 19972
  117.1 32.1 %slice-start = ((s8[11075584]{0:T(1024)(128)(4,1)}), s8[4194304]{0:T(1024)(128)(4,1)S(1)}, s32[]{:S(2)}) async-start(s8[11075584]{0:T(1024)(128)(4,1)} %bitcast.8), calls=%async_computation.3 | async-start | bytes 8388608
  117.1 32.1 %slice-start.1 = ((s8[11075584]{0:T(1024)(128)(4,1)}), s8[4194304]{0:T(1024)(128)(4,1)S(1)}, s32[]{:S(2)}) async-start(s8[11075584]{0:T(1024)(128)(4,1)} %bitcast.8), calls=%async_computation.4 | async-start | bytes 8388608
  130.5 18.8 %slice-start.2 = ((s8[11075584]{0:T(1024)(128)(4,1)}), s8[2686976]{0:T(1024)(128)(4,1)S(1)}, s32[]{:S(2)}) async-start(s8[11075584]{0:T(1024)(128)(4,1)} %bitcast.8), calls=%async_computation.5 | async-start | bytes 5373952
  156.3 3.9 collective-permute-start
  163.1 40.5 %collective-permute-start.1 = (f32[256,1664]{1,0:T(8,128)}, f32[256,1664]{1,0:T(8,128)S(1)}, u32[]{:S(2)}, u32[]{:S(2)}) collective-permute-start(f32[256,1664]{1,0:T(8,128)} %add_select_fusion.2), channel_id=1, source_target_pairs={{0,2},{2,0},{1,3},{3,1},{4,6},{6,4},{5,7},{7,5},{8,10},{10,8},{9,1... | collective-permute-start | bytes 5111816 | tf_op jit(solution)/shard_map/ppermute | solution.py:16
  205.3 38.9 %collective-permute-start.2 = (f32[256,1664]{1,0:T(8,128)S(1)}, f32[256,1664]{1,0:T(8,128)}, u32[]{:S(2)}, u32[]{:S(2)}) collective-permute-start(f32[256,1664]{1,0:T(8,128)S(1)} %add_select_fusion.1), channel_id=1, source_target_pairs={{0,4},{4,0},{1,5},{5,1},{2,6},{6,2},{3,7},{7,3},{8,12},{12,8},{9,1... | collective-permute-start | bytes 5111816 | tf_op jit(solution)/shard_map/ppermute | solution.py:16
  245.8 75.3 %collective-permute-start.3 = (f32[256,1664]{1,0:T(8,128)S(1)}, f32[256,1664]{1,0:T(8,128)S(1)}, u32[]{:S(2)}, u32[]{:S(2)}) collective-permute-start(f32[256,1664]{1,0:T(8,128)S(1)} %add_select_fusion), channel_id=1, source_target_pairs={{0,8},{8,0},{1,9},{9,1},{2,10},{10,2},{3,11},{11,3},{4,12},{12,4},... | collective-permute-start | bytes 5111816 | tf_op jit(solution)/shard_map/ppermute | solution.py:16
  335.9 105.8 %copy-start.1 = (f32[512]{0:T(512)S(1)}, f32[512]{0:T(512)}, u32[]{:S(2)}) copy-start(f32[512]{0:T(512)} %param.17) | copy-start | bytes 6148
Sparse Core Ops, SparseCore 0:
  9.5 55.9 all-gather.1
  336.0 105.6 reduce-scatter.1
where the time goes:
time: 452 us; the launch traced here: 450 us
  waiting for transfers between devices  257 us (57%)
  local copies, waits for them, and re-layouts  72 us (16%)
  matrix products  53.9 us (12%)
  other arithmetic  45.7 us (10%)
  between operations  13.5 us (3%)
  starting transfers between devices  8 us (2%)
    ppermute x4, waiting for transfers between devices, partner_2(): return lax.ppermute(block, axis, route)  151 us
    reduce_scatter x1, waiting for transfers between devices, shards(): lax.psum_scatter(partials, 'tensor', scatter_dimension=1, tiled=True)  106 us
    mul x1, local copies, waits for them, and re-layouts, shards(): local_mixer = jnp.kron(sign_table(local_order), odd_factor.T)  71 us
    mul x1, other arithmetic, shards(): local_mixer = jnp.kron(sign_table(local_order), odd_factor.T)  34.5 us
    dot_general x1, matrix products, shards(): jnp.dot(normed, up_levels, preferred_element_type=jnp.float32) * up_scale  18.8 us
    dot_general x1, matrix products, shards(): partials = jnp.dot(rotated, down_levels, preferred_element_type=jnp.float32)  14.8 us
    dot_general x1, matrix products, shards(): jnp.dot(normed, gate_levels, preferred_element_type=jnp.float32)  13.3 us
  transfers between devices with their start and end apart: 6, of which 5 were waited for; matrix products, arithmetic and copies ran while one was open for 24% of the time, Pallas kernels for 0%

commit v1 on v0

--- a/solution.py
+++ b/solution.py
@@ -1,9 +1,465 @@
+import functools
 import math
 
 import jax
 import jax.numpy as jnp
+import numpy as np
 from jax import lax
+from jax.experimental import pallas as pl
+from jax.experimental.pallas import tpu as pltpu
 from jax.sharding import PartitionSpec as P
+
+F32 = jnp.float32
+BF16 = jnp.bfloat16
+MESH = pl.DeviceIdType.MESH
+
+ORDER = (0, 2, 4, 8, 6, 12, 10, 14)
+ONWARD = (
+    ((0, 8), (0, 4), (0, 2), (0, 1)),
+    ((2, 1),),
+    ((4, 2), (4, 1)),
+    ((8, 4), (8, 2), (8, 1)),
+    ((6, 1),),
+    ((12, 2), (12, 1)),
+    ((10, 1),),
+    ((14, 1),),
+)
+RING = 5
+DOWN_RING = 8
+
+
+def pick(index, table):
+    value = jnp.int32(table[0])
+    for place, entry in enumerate(table[1:], 1):
+        value = jnp.where(index == place, jnp.int32(entry), value)
+    return value
+
+
+def fused_kernel(
+    n,
+    odd_order,
+    splits,
+    walsh_scale,
+    tokens,
+    gain,
+    gate_hbm,
+    gate_scale,
+    up_hbm,
+    up_scale,
+    odd_t,
+    down_hbm,
+    down_scale,
+    ones_row,
+    ones_col,
+    sign_row,
+    sign_col,
+    out,
+    tok,
+    square,
+    gate_w,
+    up_w,
+    down_w,
+    gate_acc,
+    up_acc,
+    mixer,
+    hid,
+    arrived,
+    rot_out,
+    rot_in,
+    kept,
+    core_out,
+    core_in,
+    x_out,
+    x_in,
+    z_out,
+    z_in,
+    gate_sem,
+    up_sem,
+    down_sem,
+    tok_send,
+    tok_recv,
+    hid_send,
+    hid_recv,
+    rot_send,
+    rot_recv,
+    core_send,
+    core_recv,
+    x_send,
+    x_recv,
+    z_send,
+    z_recv,
+):
+    me = lax.axis_index("tensor")
+    rows, depth = tokens.shape
+    width = gate_acc.shape[1]
+    share = rows // n
+    steps = 2 * len(ORDER)
+
+    def remote(source, target, offset, send, recv):
+        return pltpu.make_async_remote_copy(
+            src_ref=source,
+            dst_ref=target,
+            send_sem=send,
+            recv_sem=recv,
+            device_id={"tensor": jnp.bitwise_xor(me, offset)},
+            device_id_type=MESH,
+        )
+
+    def weight_copies(step):
+        offset = pick(step // 2, ORDER) + step % 2
+        start = pl.multiple_of(jnp.bitwise_xor(me, offset) * depth, depth)
+        slot = lax.rem(step, RING)
+        return (
+            pltpu.make_async_copy(gate_hbm.at[pl.ds(start, depth), :], gate_w.at[slot], gate_sem.at[slot]),
+            pltpu.make_async_copy(up_hbm.at[pl.ds(start, depth), :], up_w.at[slot], up_sem.at[slot]),
+        )
+
+    def start_weights(step, carry=None):
+        for copy in weight_copies(step):
+            copy.start()
+        return carry
+
+    def down_copy(step):
+        owner = jnp.bitwise_xor(me, steps - 1 - step)
+        start = pl.multiple_of(owner * depth, depth)
+        slot = lax.rem(step, DOWN_RING)
+        return pltpu.make_async_copy(down_hbm.at[:, pl.ds(start, depth)], down_w.at[slot], down_sem.at[slot])
+
+    lax.fori_loop(0, RING, lambda s, c: start_weights(jnp.int32(s), c), 0)
+
+    barrier = pltpu.get_barrier_semaphore()
+
+    def greet(offset, carry):
+        pl.semaphore_signal(
+            barrier, inc=1, device_id={"tensor": jnp.bitwise_xor(me, offset)}, device_id_type=MESH
+        )
+        return carry
+
+    lax.fori_loop(1, n, greet, 0)
+    tok[0] = tokens[...]
+    pl.semaphore_wait(barrier, n - 1)
+
+    def pass_on(block, offset):
+        landing = block ^ offset
+        return remote(tok.at[block], tok.at[landing], offset, tok_send.at[landing], tok_recv.at[landing])
+
+    def wait_block(landing):
+        remote(tok.at[landing], tok.at[landing], 1, tok_send.at[landing], tok_recv.at[landing]).wait_recv()
+
+    for block, offset in ONWARD[0]:
+        pass_on(block, offset).start()
+
+    def build(tile, carry):
+        at = pl.ds(pl.multiple_of(tile * 128, 128), 128)
+        factor_rows = jnp.dot(ones_row[at, :], odd_t[...], preferred_element_type=F32).astype(BF16)
+        factor = jnp.dot(factor_rows, ones_col[...], preferred_element_type=F32)
+        signs = jnp.dot(sign_row[at, :], sign_col[...], preferred_element_type=F32)
+        mixer[at, :] = (factor * signs).astype(BF16)
+        return carry
+
+    lax.fori_loop(0, width // 128, build, 0)
+    square[...] = jnp.zeros_like(square)
+    gate_acc[...] = jnp.zeros_like(gate_acc)
+    up_acc[...] = jnp.zeros_like(up_acc)
+
+    def project(step, carry):
+        pair, side = step // 2, step % 2
+        for place, moves in enumerate(ONWARD):
+            if place > 0:
+
+                @pl.when((pair == place) & (side == 0))
+                def _(moves=moves):
+                    wait_block(moves[0][0])
+                    for block, offset in moves:
+                        pass_on(block, offset).start()
+
+        offset = pick(pair, ORDER) + side
+
+        @pl.when(side == 1)
+        def _():
+            wait_block(offset)
+
+        for copy in weight_copies(step):
+            copy.wait()
+        slot = lax.rem(step, RING)
+        block = tok[offset].astype(F32)
+        part = square[...]
+        for lane in range(0, depth, 128):
+            piece = block[:, lane : lane + 128]
+            part = part + piece * piece
+        square[...] = part
+        scaled = (block * gain[jnp.bitwise_xor(me, offset)]).astype(BF16)
+        gate_acc[...] += jnp.dot(scaled, gate_w[slot], preferred_element_type=F32)
+        up_acc[...] += jnp.dot(scaled, up_w[slot], preferred_element_type=F32)
+
+        @pl.when(step + RING < steps)
+        def _():
+            start_weights(step + RING)
+
+        return carry
+
+    lax.fori_loop(0, steps, project, 0)
+
+    def start_down(step, carry):
+        down_copy(step).start()
+        return carry
+
+    lax.fori_loop(0, DOWN_RING, lambda s, c: start_down(jnp.int32(s), c), 0)
+
+    def rows_of(device):
+        return pl.ds(pl.multiple_of(device * share, share), share)
+
+    def exchange(source, target, part, offset, send, recv):
+        first, size = splits[part]
+        cut = pl.ds(first, size)
+        peer = jnp.bitwise_xor(me, offset)
+        return remote(
+            source.at[rows_of(peer), cut],
+            target.at[rows_of(me), cut],
+            offset,
+            send.at[part, offset],
+            recv.at[part, offset],
+        )
+
+    def each_peer(act):
+        def one(index, carry):
+            act(n - index)
+            return carry
+
+        lax.fori_loop(1, n, one, 0)
+
+    mean = jnp.sum(square[...], axis=1, keepdims=True) * (1.0 / (n * depth))
+    inverse = lax.rsqrt(mean + 1e-05)
+
+    for part, (first, size) in enumerate(splits):
+
+        def activate(tile, carry, first=first):
+            at = pl.ds(pl.multiple_of(first + tile * 128, 128), 128)
+            gate = gate_acc[:, at] * inverse * gate_scale[:, at]
+            up = up_acc[:, at] * inverse * up_scale[:, at]
+            hid[:, at] = (gate / (1.0 + jnp.exp(-gate)) * up).astype(BF16)
+            return carry
+
+        lax.fori_loop(0, size // 128, activate, 0)
+        each_peer(lambda j, part=part: exchange(hid, arrived, part, j, hid_send, hid_recv).start())
+    arrived[rows_of(me), :] = hid[rows_of(me), :]
+    for part in range(len(splits)):
+        each_peer(lambda j, part=part: exchange(hid, arrived, part, j, hid_send, hid_recv).wait_recv())
+
+    def mix(first, size):
+        at = pl.ds(first, size)
+        flat = jnp.dot(arrived[...], mixer[:, at], preferred_element_type=F32)
+        terms = [flat[i * share : (i + 1) * share] for i in range(n)]
+        bit = 1
+        while bit < n:
+            terms = [
+                terms[i ^ bit] - terms[i] if i & bit else terms[i] + terms[i ^ bit] for i in range(n)
+            ]
+            bit *= 2
+        for i in range(n):
+            rot_out[i * share : (i + 1) * share, at] = (terms[i] * walsh_scale).astype(BF16)
+
+    for part, (first, size) in enumerate(splits):
+
+        def mix_tile(tile, carry, first=first):
+            mix(pl.multiple_of(first + tile * 256, 256), 256)
+            return carry
+
+        lax.fori_loop(0, size // 256, mix_tile, 0)
+        if size % 256:
+            mix(first + size // 256 * 256, size % 256)
+        each_peer(lambda j, part=part: exchange(rot_out, rot_in, part, j, rot_send, rot_recv).start())
+    rot_in[rows_of(me), :] = rot_out[rows_of(me), :]
+    for part in range(len(splits)):
+        each_peer(lambda j, part=part: exchange(rot_out, rot_in, part, j, rot_send, rot_recv).wait_recv())
+
+    groups = steps // 2
+
+    def down_block(step):
+        down_copy(step).wait()
+        value = jnp.dot(rot_in[...], down_w[lax.rem(step, DOWN_RING)], preferred_element_type=F32)
+        return value
+
+    def refill(step):
+        @pl.when(step + DOWN_RING < steps)
+        def _():
+            down_copy(step + DOWN_RING).start()
+
+    def to_core(group):
+        return remote(core_out.at[group], core_in.at[group], 1, core_send.at[group], core_recv.at[group])
+
+    def to_x(turn):
+        return remote(x_out.at[turn], x_in.at[turn], 2, x_send.at[turn], x_recv.at[turn])
+
+    def to_z(turn, offset):
+        return remote(z_out.at[turn], z_in.at[turn], offset, z_send.at[turn], z_recv.at[turn])
+
+    def combine(group):
+        to_core(group).wait_recv()
+        total = kept[group] + core_in[group].astype(F32)
+        turn = group // 2
+
+        @pl.when(group % 2 == 0)
+        def _():
+            x_out[turn] = total.astype(BF16)
+            to_x(turn).start()
+
+        @pl.when(group % 2 == 1)
+        def _():
+            kept[group] = total
+
+    def lower(group, carry):
+        core_out[group] = down_block(2 * group).astype(BF16)
+        to_core(group).start()
+        refill(2 * group)
+        kept[group] = down_block(2 * group + 1)
+        refill(2 * group + 1)
+
+        @pl.when(group > 0)
+        def _():
+            combine(group - 1)
+
+        return carry
+
+    lax.fori_loop(0, groups, lambda g, c: lower(jnp.int32(g), c), 0)
+    combine(jnp.int32(groups - 1))
+
+    to_x(0).wait_recv()
+    z_out[0] = (kept[1] + x_in[0].astype(F32)).astype(BF16)
+    to_z(0, 4).start()
+    to_x(1).wait_recv()
+    to_z(0, 4).wait_recv()
+    z_out[1] = (kept[3] + x_in[1].astype(F32) + z_in[0].astype(F32)).astype(BF16)
+    to_z(1, 8).start()
+    to_x(2).wait_recv()
+    z_out[2] = (kept[5] + x_in[2].astype(F32)).astype(BF16)
+    to_z(2, 4).start()
+    to_x(3).wait_recv()
+    to_z(1, 8).wait_recv()
+    total = kept[7] + x_in[3].astype(F32) + z_in[1].astype(F32)
+    to_z(2, 4).wait_recv()
+    out[...] = ((total + z_in[2].astype(F32)) * down_scale[...]).astype(BF16)
+
+    for moves in ONWARD:
+        for block, offset in moves:
+            pass_on(block, offset).wait_send()
+    for part in range(len(splits)):
+        each_peer(lambda j, part=part: exchange(hid, arrived, part, j, hid_send, hid_recv).wait_send())
+        each_peer(lambda j, part=part: exchange(rot_out, rot_in, part, j, rot_send, rot_recv).wait_send())
+
+    def finish(group, carry):
+        to_core(group).wait_send()
+        return carry
+
+    lax.fori_loop(0, groups, finish, 0)
+    for turn in range(4):
+        to_x(turn).wait_send()
+    for turn, offset in ((0, 4), (1, 8), (2, 4)):
+        to_z(turn, offset).wait_send()
+
+
+def small_signs(order):
+    indices = np.arange(order)
+    common = indices[:, None] & indices[None, :]
+    parity = np.zeros_like(common)
+    while common.any():
+        parity ^= common & 1
+        common >>= 1
+    return 1.0 - 2.0 * parity
+
+
+def fused_shards(
+    tokens,
+    norm_gain,
+    gate_levels,
+    gate_scale,
+    up_levels,
+    up_scale,
+    odd_factor,
+    down_levels,
+    down_scale,
+):
+    n = lax.axis_size("tensor")
+    rows, depth = tokens.shape
+    width = gate_levels.shape[1]
+    odd_order = odd_factor.shape[0]
+    order = width // odd_order
+    units = np.arange(width)
+    ones = np.zeros((width, 128), np.float32)
+    ones[units, units % odd_order] = 1.0
+    owners = np.zeros((width, order), np.float32)
+    owners[units, units // odd_order] = 1.0
+    signs = owners @ small_signs(order)
+    constants = [jnp.asarray(a, BF16) for a in (ones, ones.T, signs, owners.T)]
+    odd_t = jnp.pad(odd_factor.T, ((0, 128 - odd_order),) * 2).astype(BF16)
+    half = width // 2 // 256 * 256
+    splits = ((0, half), (half, width - half))
+    vmem = pl.BlockSpec(memory_space=pltpu.VMEM)
+    hbm = pl.BlockSpec(memory_space=pl.ANY)
+    dma = pltpu.SemaphoreType.DMA
+    block = (rows, depth)
+    kernel = functools.partial(fused_kernel, n, odd_order, splits, 1.0 / math.sqrt(order * n))
+    return pl.pallas_call(
+        kernel,
+        out_shape=jax.ShapeDtypeStruct(block, BF16),
+        in_specs=[vmem, vmem, hbm, vmem, hbm, vmem, vmem, hbm, vmem] + [vmem] * 4,
+        out_specs=vmem,
+        scratch_shapes=[
+            pltpu.VMEM((n,) + block, BF16),
+            pltpu.VMEM((rows, 128), F32),
+            pltpu.VMEM((RING, depth, width), BF16),
+            pltpu.VMEM((RING, depth, width), BF16),
+            pltpu.VMEM((DOWN_RING, width, depth), BF16),
+            pltpu.VMEM((rows, width), F32),
+            pltpu.VMEM((rows, width), F32),
+            pltpu.VMEM((width, width), BF16),
+            pltpu.VMEM((rows, width), BF16),
+            pltpu.VMEM((rows, width), BF16),
+            pltpu.VMEM((rows, width), BF16),
+            pltpu.VMEM((rows, width), BF16),
+            pltpu.VMEM((8,) + block, F32),
+            pltpu.VMEM((8,) + block, BF16),
+            pltpu.VMEM((8,) + block, BF16),
+            pltpu.VMEM((4,) + block, BF16),
+            pltpu.VMEM((4,) + block, BF16),
+            pltpu.VMEM((3,) + block, BF16),
+            pltpu.VMEM((3,) + block, BF16),
+            dma((RING,)),
+            dma((RING,)),
+            dma((DOWN_RING,)),
+            dma((n,)),
+            dma((n,)),
+            dma((2, n)),
+            dma((2, n)),
+            dma((2, n)),
+            dma((2, n)),
+            dma((8,)),
+            dma((8,)),
+            dma((4,)),
+            dma((4,)),
+            dma((3,)),
+            dma((3,)),
+        ],
+        compiler_params=pltpu.CompilerParams(
+            collective_id=0, has_side_effects=True, vmem_limit_bytes=64 * 1024 * 1024 - 65536
+        ),
+        cost_estimate=pl.CostEstimate(
+            flops=2 * rows * width * (3 * n * depth + width),
+            bytes_accessed=6 * n * depth * width,
+            transcendentals=rows * width,
+        ),
+    )(
+        tokens,
+        norm_gain.reshape(n, 1, depth),
+        gate_levels,
+        gate_scale.reshape(1, width),
+        up_levels,
+        up_scale.reshape(1, width),
+        odd_t,
+        down_levels,
+        down_scale.reshape(1, depth),
+        *constants,
+    )
 
 
 def partner_2(block, axis, distance):
@@ -37,6 +493,19 @@
     down_scale,
 ):
     devices = lax.axis_size("tensor")
+    order = gate_levels.shape[1] // odd_factor.shape[0]
+    if devices == 16 and order == 128 and tokens.shape[1] % 128 == 0 and tokens.shape[0] % 256 == 0:
+        return fused_shards(
+            tokens,
+            norm_gain,
+            gate_levels,
+            gate_scale,
+            up_levels,
+            up_scale,
+            odd_factor,
+            down_levels,
+            down_scale,
+        )
     gathered = lax.all_gather(tokens, "tensor", axis=1, tiled=True)
     floats = gathered.astype(jnp.float32)
     inverse = lax.rsqrt(jnp.mean(floats * floats, axis=1, keepdims=True) + 1e-05)

time: 452 us -> 123 us (0.27)
  waiting for transfers between devices: 257 us -> 0 us
  Pallas kernels: 0 us -> 117 us
  local copies, waits for them, and re-layouts: 72 us -> 5.67 us
  matrix products: 53.9 us -> 0 us
  other arithmetic: 45.7 us -> 0 us
  between operations: 13.5 us -> 0.01 us
  starting transfers between devices: 8 us -> 0 us
    ppermute x4 -> x0, waiting for transfers between devices: 151 us -> none  [partner_2(): return lax.ppermute(block, axis, route)]
    pallas_call x0 -> x1, Pallas kernels: none -> 117 us  [fused_shards(): pl.pallas_call(kernel, out_shape=jax.ShapeDtypeStruct(block, BF16), in_sp...]
    reduce_scatter x1 -> x0, waiting for transfers between devices: 106 us -> none  [shards(): lax.psum_scatter(partials, 'tensor', scatter_dimension=1, tiled=True)]
    mul x1 -> x0, local copies, waits for them, and re-layouts: 71 us -> none  [shards(): local_mixer = jnp.kron(sign_table(local_order), odd_factor.T)]
    dot_general x4 -> x0, matrix products: 53.9 us -> none  [the longest x1 18.8 us: shards(): jnp.dot(normed, up_levels, preferred_element_type=jnp.float32) * up_scale]
    mul x1 -> x0, other arithmetic: 34.5 us -> none  [shards(): local_mixer = jnp.kron(sign_table(local_order), odd_factor.T)]
    ppermute x4 -> x0, starting transfers between devices: 7.96 us -> none  [partner_2(): return lax.ppermute(block, axis, route)]
    select_n x3 -> x0, other arithmetic: 6.09 us -> none  [shards(): spread = jnp.where(is_upper, partner - spread, spread + partner)]
  transfers between devices with their start and end apart: 6 -> 0, of which waited for: 5 -> 0; matrix products, arithmetic and copies ran while one was open for 24% -> 0% of each run, Pallas kernels for 0% -> 0%
where the time goes in v1:
time: 123 us
  Pallas kernels  117 us (95%)
  local copies, waits for them, and re-layouts  5.67 us (5%)
    pallas_call x1, Pallas kernels, fused_shards(): pl.pallas_call(kernel, out_shape=jax.ShapeDtypeStruct(block, BF16), in_sp...  117 us

profile of v1, /device:TPU:0, one launch (start us, length us, event | category | flops | bytes accessed | tf_op | source)
XLA Modules:
  0.0 123.0 jit_solution(11255892581099073294)
XLA Ops:
  0.0 0.8 copy.14
  0.8 1.3 %reshape.13.gate_scale = f32[1,1664]{1,0:T(1,128)} reshape(f32[1664]{0:T(1024)} %param.16) | data formatting | bytes 13312 | tf_op jit(solution)/shard_map/reshape | solution.py:455
  2.1 1.3 %reshape.14.up_scale = f32[1,1664]{1,0:T(1,128)} reshape(f32[1664]{0:T(1024)} %param.18) | data formatting | bytes 13312 | tf_op jit(solution)/shard_map/reshape | solution.py:457
  3.4 0.6 pad.5.odd_t
  4.0 117.3 %shard_map.127 = bf16[256,512]{1,0:T(8,128)(2,1)} custom-call(bf16[256,512]{1,0:T(8,128)(2,1)} %tokens.1, f32[16,1,512]{2,1,0:T(1,128)} %bitcast.5, bf16[8192,1664]{1,0:T(8,128)(2,1)} %gate_hbm.1, f32[1,1664]{1,0:T(1,128)} %reshape.13.gate_scale, bf16[8192,1664]{1,0:T(8,128)(2,1)} %up_hbm.1, f32[1,1664]{1,0:T(1,128)} %reshape.14.up_scale, ...), custom_call_target="tpu_custom_call" | custom-call | flops 22355640320 | bytes 81788928 | tf_op jit(solution)/shard_map/pallas_call | solution.py:402
  121.3 1.7 %copy.16 = bf16[256,512]{1,0:T(8,128)(2,1)} copy(bf16[256,512]{1,0:T(8,128)(2,1)} %shard_map.127) | data formatting | bytes 524288

commit v2 on v1

--- a/solution.py
+++ b/solution.py
@@ -43,19 +43,27 @@
     tokens,
     gain,
     gate_hbm,
-    gate_scale,
+    gate_scale_1d,
     up_hbm,
-    up_scale,
-    odd_t,
+    up_scale_1d,
+    odd,
     down_hbm,
     down_scale,
+    ones_row_hbm,
+    ones_col_hbm,
+    sign_row_hbm,
+    sign_col_hbm,
+    out,
+    tok,
+    inverse,
+    gate_scale,
+    up_scale,
+    sums,
+    odd_pad,
     ones_row,
     ones_col,
     sign_row,
     sign_col,
-    out,
-    tok,
-    square,
     gate_w,
     up_w,
     down_w,
@@ -76,6 +84,9 @@
     gate_sem,
     up_sem,
     down_sem,
+    sums_send,
+    sums_recv,
+    const_sem,
     tok_send,
     tok_recv,
     hid_send,
@@ -127,6 +138,20 @@
 
     lax.fori_loop(0, RING, lambda s, c: start_weights(jnp.int32(s), c), 0)
 
+    constant_copies = [
+        pltpu.make_async_copy(source, target, const_sem.at[i])
+        for i, (source, target) in enumerate(
+            (
+                (ones_row_hbm, ones_row),
+                (ones_col_hbm, ones_col),
+                (sign_row_hbm, sign_row),
+                (sign_col_hbm, sign_col),
+            )
+        )
+    ]
+    for copy in constant_copies:
+        copy.start()
+
     barrier = pltpu.get_barrier_semaphore()
 
     def greet(offset, carry):
@@ -137,6 +162,17 @@
 
     lax.fori_loop(1, n, greet, 0)
     tok[0] = tokens[...]
+    own = tokens[...].astype(F32)
+    part = jnp.zeros((rows, 128), F32)
+    for lane in range(0, depth, 128):
+        part = part + own[:, lane : lane + 128] * own[:, lane : lane + 128]
+    sums[0] = lax.dot_general(
+        jnp.ones((8, 128), F32),
+        part,
+        (((1,), (1,)), ((), ())),
+        precision=lax.Precision.HIGHEST,
+        preferred_element_type=F32,
+    )
     pl.semaphore_wait(barrier, n - 1)
 
     def pass_on(block, offset):
@@ -146,21 +182,37 @@
     def wait_block(landing):
         remote(tok.at[landing], tok.at[landing], 1, tok_send.at[landing], tok_recv.at[landing]).wait_recv()
 
+    def sums_to(j):
+        return remote(sums.at[0], sums.at[j], j, sums_send.at[j], sums_recv.at[j])
+
+    def each_peer(act):
+        def one(index, carry):
+            act(n - index)
+            return carry
+
+        lax.fori_loop(1, n, one, 0)
+
+    each_peer(lambda j: sums_to(j).start())
     for block, offset in ONWARD[0]:
         pass_on(block, offset).start()
-
-    def build(tile, carry):
-        at = pl.ds(pl.multiple_of(tile * 128, 128), 128)
-        factor_rows = jnp.dot(ones_row[at, :], odd_t[...], preferred_element_type=F32).astype(BF16)
-        factor = jnp.dot(factor_rows, ones_col[...], preferred_element_type=F32)
-        signs = jnp.dot(sign_row[at, :], sign_col[...], preferred_element_type=F32)
-        mixer[at, :] = (factor * signs).astype(BF16)
-        return carry
-
-    lax.fori_loop(0, width // 128, build, 0)
-    square[...] = jnp.zeros_like(square)
+    gate_scale[...] = gate_scale_1d[...].reshape(1, width)
+    up_scale[...] = up_scale_1d[...].reshape(1, width)
+
     gate_acc[...] = jnp.zeros_like(gate_acc)
     up_acc[...] = jnp.zeros_like(up_acc)
+
+    each_peer(lambda j: sums_to(j).wait_recv())
+    total = sums[0]
+    for j in range(1, n):
+        total = total + sums[j]
+    spread = lax.dot_general(
+        total,
+        jnp.full((8, 128), 0.125, F32),
+        (((0,), (0,)), ((), ())),
+        precision=lax.Precision.HIGHEST,
+        preferred_element_type=F32,
+    )
+    inverse[...] = lax.rsqrt(spread * (1.0 / (n * depth)) + 1e-05)
 
     def project(step, carry):
         pair, side = step // 2, step % 2
@@ -183,12 +235,8 @@
             copy.wait()
         slot = lax.rem(step, RING)
         block = tok[offset].astype(F32)
-        part = square[...]
-        for lane in range(0, depth, 128):
-            piece = block[:, lane : lane + 128]
-            part = part + piece * piece
-        square[...] = part
-        scaled = (block * gain[jnp.bitwise_xor(me, offset)]).astype(BF16)
+        factor = jnp.concatenate([inverse[...]] * (depth // 128), axis=1)
+        scaled = (block * factor * gain[jnp.bitwise_xor(me, offset)]).astype(BF16)
         gate_acc[...] += jnp.dot(scaled, gate_w[slot], preferred_element_type=F32)
         up_acc[...] += jnp.dot(scaled, up_w[slot], preferred_element_type=F32)
 
@@ -221,27 +269,33 @@
             recv.at[part, offset],
         )
 
-    def each_peer(act):
-        def one(index, carry):
-            act(n - index)
-            return carry
-
-        lax.fori_loop(1, n, one, 0)
-
-    mean = jnp.sum(square[...], axis=1, keepdims=True) * (1.0 / (n * depth))
-    inverse = lax.rsqrt(mean + 1e-05)
-
     for part, (first, size) in enumerate(splits):
 
         def activate(tile, carry, first=first):
             at = pl.ds(pl.multiple_of(first + tile * 128, 128), 128)
-            gate = gate_acc[:, at] * inverse * gate_scale[:, at]
-            up = up_acc[:, at] * inverse * up_scale[:, at]
+            gate = gate_acc[:, at] * gate_scale[:, at]
+            up = up_acc[:, at] * up_scale[:, at]
             hid[:, at] = (gate / (1.0 + jnp.exp(-gate)) * up).astype(BF16)
             return carry
 
         lax.fori_loop(0, size // 128, activate, 0)
         each_peer(lambda j, part=part: exchange(hid, arrived, part, j, hid_send, hid_recv).start())
+    odd_pad[...] = jnp.zeros_like(odd_pad)
+    odd_pad[0:odd_order, 0:odd_order] = odd[...]
+    for copy in constant_copies:
+        copy.wait()
+
+    def build(tile, carry):
+        at = pl.ds(pl.multiple_of(tile * 128, 128), 128)
+        factor_rows = lax.dot_general(
+                ones_row[at, :], odd_pad[...].astype(BF16), (((1,), (1,)), ((), ())), preferred_element_type=F32
+            ).astype(BF16)
+        factor = jnp.dot(factor_rows, ones_col[...], preferred_element_type=F32)
+        signs = jnp.dot(sign_row[at, :], sign_col[...], preferred_element_type=F32)
+        mixer[at, :] = (factor * signs).astype(BF16)
+        return carry
+
+    lax.fori_loop(0, width // 128, build, 0)
     arrived[rows_of(me), :] = hid[rows_of(me), :]
     for part in range(len(splits)):
         each_peer(lambda j, part=part: exchange(hid, arrived, part, j, hid_send, hid_recv).wait_recv())
@@ -343,6 +397,7 @@
     for moves in ONWARD:
         for block, offset in moves:
             pass_on(block, offset).wait_send()
+    each_peer(lambda j: sums_to(j).wait_send())
     for part in range(len(splits)):
         each_peer(lambda j, part=part: exchange(hid, arrived, part, j, hid_send, hid_recv).wait_send())
         each_peer(lambda j, part=part: exchange(rot_out, rot_in, part, j, rot_send, rot_recv).wait_send())
@@ -391,7 +446,6 @@
     owners[units, units // odd_order] = 1.0
     signs = owners @ small_signs(order)
     constants = [jnp.asarray(a, BF16) for a in (ones, ones.T, signs, owners.T)]
-    odd_t = jnp.pad(odd_factor.T, ((0, 128 - odd_order),) * 2).astype(BF16)
     half = width // 2 // 256 * 256
     splits = ((0, half), (half, width - half))
     vmem = pl.BlockSpec(memory_space=pltpu.VMEM)
@@ -402,11 +456,19 @@
     return pl.pallas_call(
         kernel,
         out_shape=jax.ShapeDtypeStruct(block, BF16),
-        in_specs=[vmem, vmem, hbm, vmem, hbm, vmem, vmem, hbm, vmem] + [vmem] * 4,
+        in_specs=[vmem, vmem, hbm, vmem, hbm, vmem, vmem, hbm, vmem] + [hbm] * 4,
         out_specs=vmem,
         scratch_shapes=[
             pltpu.VMEM((n,) + block, BF16),
             pltpu.VMEM((rows, 128), F32),
+            pltpu.VMEM((1, width), F32),
+            pltpu.VMEM((1, width), F32),
+            pltpu.VMEM((n, 8, rows), F32),
+            pltpu.VMEM((128, 128), F32),
+            pltpu.VMEM((width, 128), BF16),
+            pltpu.VMEM((128, width), BF16),
+            pltpu.VMEM((width, 128), BF16),
+            pltpu.VMEM((128, width), BF16),
             pltpu.VMEM((RING, depth, width), BF16),
             pltpu.VMEM((RING, depth, width), BF16),
             pltpu.VMEM((DOWN_RING, width, depth), BF16),
@@ -427,6 +489,9 @@
             dma((RING,)),
             dma((RING,)),
             dma((DOWN_RING,)),
+            dma((n,)),
+            dma((n,)),
+            dma((4,)),
             dma((n,)),
             dma((n,)),
             dma((2, n)),
@@ -452,10 +517,10 @@
         tokens,
         norm_gain.reshape(n, 1, depth),
         gate_levels,
-        gate_scale.reshape(1, width),
+        gate_scale,
         up_levels,
-        up_scale.reshape(1, width),
-        odd_t,
+        up_scale,
+        odd_factor,
         down_levels,
         down_scale.reshape(1, depth),
         *constants,

time: 123 us -> 121 us (0.984)
  local copies, waits for them, and re-layouts: 5.67 us -> 1.67 us
  Pallas kernels: 117 us -> 120 us
    reshape x2 -> x0, local copies, waits for them, and re-layouts: 2.6 us -> none  [the longest x1 1.31 us: fused_shards(): gate_scale.reshape(1, width)]
    pallas_call x1, Pallas kernels: 117 us -> 120 us  [fused_shards(): pl.pallas_call(kernel, out_shape=jax.ShapeDtypeStruct(block, BF16), in_sp...]
where the time goes in v2:
time: 121 us
  Pallas kernels  120 us (99%)
  local copies, waits for them, and re-layouts  1.67 us (1%)
    pallas_call x1, Pallas kernels, fused_shards(): pl.pallas_call(kernel, out_shape=jax.ShapeDtypeStruct(block, BF16), in_sp...  120 us

profile of v2, /device:TPU:0, one launch (start us, length us, event | category | flops | bytes accessed | tf_op | source)
XLA Modules:
  0.0 121.3 jit_solution(17499855296401296390)
XLA Ops:
  0.0 119.6 %shard_map.127 = bf16[256,512]{1,0:T(8,128)(2,1)} custom-call(bf16[256,512]{1,0:T(8,128)(2,1)} %tokens.1, f32[16,1,512]{2,1,0:T(1,128)} %bitcast.2, bf16[8192,1664]{1,0:T(8,128)(2,1)} %gate_hbm.1, f32[1664]{0:T(1024)} %gate_scale_1d.1, bf16[8192,1664]{1,0:T(8,128)(2,1)} %up_hbm.1, f32[1664]{0:T(1024)} %up_scale_1d.1, f32[13,13]{1,0:T(8,128)} %odd.1, ...), custom_call_target="tpu_custom_call" | custom-call | flops 22355640320 | bytes 81788928 | tf_op jit(solution)/shard_map/pallas_call | solution.py:456
  119.7 1.7 %copy.15 = bf16[256,512]{1,0:T(8,128)(2,1)} copy(bf16[256,512]{1,0:T(8,128)(2,1)} %shard_map.127) | data formatting | bytes 524288
